TPU v7x, 32 devices: a whole 2x2x4 slice. The times are simulated.
32 devices in a mesh: group: 1, ctx: 32 (over z, y, x, core), tp: 1.
Axes of the slice: x: 2, y: 2, z: 4, core: 2. Of those that a mesh axis runs over, the one named last changes fastest.
Arguments:
- hidden_in: bfloat16 [4096, 4096], P(('group', 'ctx'), 'tp'), may hold values from -6 to 6
- route: int32 [4096], P(('group', 'ctx')), may hold values from 0 to 4095, as said below
- queries: bfloat16 [4096, 768], P(('group', 'ctx'), 'tp'), may hold values from -400 to 400
- keys_values: bfloat16 [4096, 256], P(('group', 'ctx')), may hold values from -5 to 5
- ancestors: int32 [32, 16], P(('group', 'ctx')), may hold values from -1 to 31, as said below
- segments: int32 [4096], P(('group', 'ctx')), may hold values from 0 to 127, never falling along the last dimension, each value on 1 to 64 neighbouring positions
- w_out: bfloat16 [768, 4096], P('tp'), may hold values from -0.21875 to 0.21875
- w_score: float32 [4096], P('tp'), may hold values from -0.09375 to 0.09375
Outputs:
- hidden_out: bfloat16 [4096, 4096], P(('group', 'ctx'), 'tp')
- token_scores: float32 [4096], P(('group', 'ctx'))
Inputs may be any that keep to these rules, and one draw needn't show every extreme that they name: route is a permutation of the context positions. The 128 rows of one loader shard send at most 5 rows to each context shard (positions of one block of 128), and some pair reaches 5; each context shard receives 128 rows. Within a context shard, positions follow the loader shard's index and then the row's index in it. `ancestors`: row b lists 1 to 16 distinct blocks other than b, then -1 to the end; some row lists 16.
All inputs are finite; a program needn't handle non-finite values.
Results may differ from a plain program's by a relative error of at most 0.005.
Values may be sent and summed in bfloat16 or wider, within the bound.
A program may use at most 64 MiB of HBM per device.

v0:
```python
import math

import jax
import jax.numpy as jnp
from jax import lax
from jax.sharding import PartitionSpec as P

HEAD = 128
BLOCK = 128


neg_big = -1e30
window_shards = 4


def passed_along(block, axis, distance):
    devices = range(lax.axis_size(axis))
    route = [((i - distance) % len(devices), i) for i in devices]
    return lax.ppermute(block, axis, route)


def online_update(soft_state, query_rows, kv_rows, visible):
    run_max, run_sum, run_acc = soft_state
    head_size = kv_rows.shape[1] // 2
    logits = jnp.einsum(
        "thd,kd->htk", query_rows, kv_rows[:, :head_size], preferred_element_type=jnp.float32
    )
    logits = jnp.where(visible[None, :, :], logits * (1.0 / math.sqrt(head_size)), neg_big)
    new_max = jnp.maximum(run_max, jnp.max(logits, axis=2))
    factor = jnp.exp(run_max - new_max)
    exp_terms = jnp.exp(logits - new_max[:, :, None])
    new_sum = run_sum * factor + jnp.sum(exp_terms, axis=2)
    weighted = jnp.einsum(
        "htk,kd->htd",
        exp_terms.astype(jnp.bfloat16),
        kv_rows[:, head_size:],
        preferred_element_type=jnp.float32,
    )
    return (new_max, new_sum, run_acc * factor[:, :, None] + weighted)


def on_device(hidden_in, route, queries, keys_values, ancestors, segments, w_out, w_score):
    tok_rows = hidden_in.shape[0]
    half_width = hidden_in.shape[1]
    ctx_count = lax.axis_size("ctx")
    capacity = (tok_rows + ctx_count - 1) // ctx_count + 1
    slot_count = ctx_count * capacity
    dest_shard = route // tok_rows
    dest_hot = (dest_shard[:, None] == jnp.arange(ctx_count, dtype=jnp.int32)[None, :]).astype(
        jnp.int32
    )
    slot_rank = jnp.sum(jnp.cumsum(dest_hot, axis=0) * dest_hot, axis=1) - 1
    slot_index = dest_shard * capacity + slot_rank
    slot_match = jnp.arange(slot_count, dtype=jnp.int32)[:, None] == slot_index[None, :]
    outgoing = jnp.dot(
        slot_match.astype(jnp.bfloat16), hidden_in, preferred_element_type=jnp.float32
    ).astype(jnp.bfloat16)
    filled = jnp.any(slot_match, axis=1).astype(jnp.bfloat16)
    arrived, arrived_flags = (
        lax.all_to_all(
            outgoing.reshape(ctx_count, capacity, half_width),
            "ctx",
            split_axis=0,
            concat_axis=0,
            tiled=True,
        ),
        lax.all_to_all(
            filled.reshape(ctx_count, capacity), "ctx", split_axis=0, concat_axis=0, tiled=True
        ),
    )
    slot_flags = arrived_flags.reshape(slot_count).astype(jnp.float32)
    local_slot = (jnp.cumsum(slot_flags) - 1.0).astype(jnp.int32)
    local_slot = jnp.where(slot_flags > 0.5, local_slot, -1)
    place_match = (jnp.arange(tok_rows, dtype=jnp.int32)[:, None] == local_slot[None, :]).astype(
        jnp.bfloat16
    )
    hidden_ctx = jnp.dot(
        place_match, arrived.reshape(slot_count, half_width), preferred_element_type=jnp.float32
    )
    query_heads = queries.shape[1] // HEAD
    query_rows = queries.reshape(tok_rows, query_heads, HEAD)
    per_shard = tok_rows // BLOCK
    positions = jnp.arange(tok_rows)
    own_mask = (
        (positions[:, None] // BLOCK == positions[None, :] // BLOCK)
        & (positions[None, :] <= positions[:, None])
        & (segments[None, :] == segments[:, None])
    )
    soft_state = (
        jnp.full((query_heads, tok_rows), neg_big, jnp.float32),
        jnp.zeros((query_heads, tok_rows), jnp.float32),
        jnp.zeros((query_heads, tok_rows, HEAD), jnp.float32),
    )
    soft_state = online_update(soft_state, query_rows, keys_values, own_mask)
    ctx_index = lax.axis_index("ctx")

    def consume(held_state, kv_rows, key_blocks):
        listed_hits = jnp.any(ancestors[:, :, None] == key_blocks[None, None, :], axis=1)
        visible = jnp.repeat(jnp.repeat(listed_hits, BLOCK, axis=0), BLOCK, axis=1)
        return online_update(held_state, query_rows, kv_rows, visible)

    def window_blocks(first_shard):
        offsets = jnp.arange(window_shards * per_shard, dtype=jnp.int32)
        shard_ids = (first_shard + offsets // per_shard) % ctx_count
        return shard_ids * per_shard + offsets % per_shard

    pieces = []
    for back_steps in (3, 2, 1):
        piece = passed_along(keys_values, "ctx", back_steps)
        pieces.append(piece)
    window = jnp.concatenate(pieces + [keys_values], axis=0)
    soft_state = consume(soft_state, window, window_blocks(ctx_index - 3))

    def step_ahead(moving):
        return passed_along(moving, "ctx", window_shards)

    def step_behind(moving):
        return passed_along(moving, "ctx", -window_shards)

    windows_total = ctx_count // window_shards
    ahead_turns = windows_total // 2
    behind_turns = (windows_total - 1) // 2

    def paired_turn(turn_index, loop_carry):
        held_state, ahead_window, behind_window = loop_carry
        ahead_window = step_ahead(ahead_window)
        behind_window = step_behind(behind_window)
        held_state = consume(
            held_state, ahead_window, window_blocks(ctx_index - 3 - window_shards * turn_index)
        )
        held_state = consume(
            held_state, behind_window, window_blocks(ctx_index - 3 + window_shards * turn_index)
        )
        return (held_state, ahead_window, behind_window)

    soft_state, ahead_window, behind_window = lax.fori_loop(
        1, behind_turns + 1, paired_turn, (soft_state, window, window)
    )
    ahead_window = step_ahead(ahead_window)
    soft_state = consume(
        soft_state, ahead_window, window_blocks(ctx_index - 3 - window_shards * ahead_turns)
    )
    run_max, run_sum, run_acc = soft_state
    attended = (run_acc / run_sum[:, :, None]).astype(jnp.bfloat16)
    partial_proj = jnp.einsum(
        "htd,hde->te",
        attended,
        w_out.reshape(query_heads, HEAD, w_out.shape[1]),
        preferred_element_type=jnp.float32,
    )
    projected = lax.psum_scatter(
        partial_proj.astype(jnp.bfloat16), "tp", scatter_dimension=1, tiled=True
    ).astype(jnp.float32)
    hidden_out = (hidden_ctx + projected).astype(jnp.bfloat16)
    score_part = jnp.sum(hidden_out.astype(jnp.float32) * w_score[None, :], axis=1)
    token_scores = lax.psum(score_part, "tp")
    return (hidden_out, token_scores)


def solution(mesh):
    placed = (
        P(("group", "ctx"), "tp"),
        P(("group", "ctx")),
        P(("group", "ctx"), "tp"),
        P(("group", "ctx"), None),
        P(("group", "ctx"), None),
        P(("group", "ctx")),
        P("tp", None),
        P("tp"),
    )
    return jax.shard_map(
        on_device,
        mesh=mesh,
        in_specs=placed,
        out_specs=(P(("group", "ctx"), "tp"), P(("group", "ctx"))),
        check_vma=False,
    )
```

profile of v0, /device:TPU:8, one launch (start us, length us, event | category | flops | bytes accessed | tf_op | source)
XLA Modules:
  0.0 131.0 jit_solution(1121825247498661413)
XLA Ops:
  0.7 1.0 collective-permute-start.2
  1.6 1.5 %collective-permute-start.3 = (bf16[128,256]{1,0:T(8,128)(2,1)}, bf16[128,256]{1,0:T(8,128)(2,1)}, u32[]{:S(2)}, u32[]{:S(2)}) collective-permute-start(bf16[128,256]{1,0:T(8,128)(2,1)} %param.13), channel_id=1, source_target_pairs={{30,0},{31,1},{0,2},{1,3},{2,4},{3,5},{4,6},{5,7},{6,8},{7,9},{8,1... | collective-permute-start | bytes 196616 | tf_op jit(solution)/shard_map/ppermute | solution.py:19
  6.2 5.8 %all-to-all-start = ((bf16[32,1,5]{2,1,0:T(2,128)(2,1)}), bf16[32,1,5]{2,1,0:T(2,128)(2,1)S(1)}, u32[]{:S(2)}, u32[]{:S(2)}) async-start(bf16[32,1,5]{2,1,0:T(2,128)(2,1)} %reshape.572), calls=%async_computation | async-start | bytes 32768 | tf_op jit(solution)/shard_map/all_to_all | solution.py:67
  12.0 1.1 copy.37
  13.2 0.9 compare_reduce_fusion.3
  15.2 1.6 %reshape.555 = bf16[32,5,4096]{2,1,0:T(8,128)(2,1)} reshape(bf16[160,4096]{1,0:T(8,128)(2,1)S(1)} %convolution_convert_fusion) | data formatting | bytes 2621440 | tf_op jit(solution)/shard_map/reshape | solution.py:61
  16.8 1.1 all-to-all-done
  17.9 4.8 %all-to-all-start.1 = ((bf16[32,5,4096]{2,1,0:T(8,128)(2,1)}), bf16[32,5,4096]{2,1,0:T(8,128)(2,1)}, u32[]{:S(2)}, u32[]{:S(2)}) async-start(bf16[32,5,4096]{2,1,0:T(8,128)(2,1)} %reshape.555), calls=%async_computation.1 | async-start | bytes 4194304 | tf_op jit(solution)/shard_map/all_to_all | solution.py:60
  23.4 0.8 constant_dynamic-update-slice_fusion.3
  24.2 0.8 constant_dynamic-update-slice_fusion.2
  26.7 82.7 %while.24 = (s32[]{:T(128)}, f32[6,128]{1,0:T(8,128)S(1)}, f32[6,128]{1,0:T(8,128)S(1)}, f32[6,128,128]{2,1,0:T(8,128)S(1)}, bf16[512,256]{1,0:T(8,128)(2,1)S(1)...) while((s32[]{:T(128)}, f32[6,128]{1,0:T(8,128)S(1)}, ...), condition=%wide.region_17.18_spmd, body=%wide.region_10.17_spmd.sunk | while | flops 408554848 | bytes 15159673 | solution.py:136
  26.7 1.5 %collective-permute-start = (bf16[512,256]{1,0:T(8,128)(2,1)S(1)}, bf16[512,256]{1,0:T(8,128)(2,1)S(1)}, u32[]{:S(2)}, u32[]{:S(2)}) collective-permute-start(bf16[512,256]{1,0:T(8,128)(2,1)S(1)} %get-tuple-element.444), channel_id=1, source_target_pairs={{4,0},{5,1},{6,2},{7,3},{8,4},{9,5},{10,6},{11,7},{12,8},{13,9},{1... | collective-permute-start | bytes 786440 | tf_op jit(solution)/shard_map/while/body/eval_jaxpr/ppermute | solution.py:19
  29.1 27.9 %collective-permute-done = bf16[512,256]{1,0:T(8,128)(2,1)S(1)} collective-permute-done((bf16[512,256]{1,0:T(8,128)(2,1)S(1)}, bf16[512,256]{1,0:T(8,128)(2,1)S(1)}, u32[]{:S(2)}, u32[]{:S(2)}) %collective-permute-start) | collective-permute-done | bytes 262176 | tf_op jit(solution)/shard_map/while/body/eval_jaxpr/ppermute | solution.py:19
  57.5 7.4 %collective-permute-done.1 = bf16[512,256]{1,0:T(8,128)(2,1)S(1)} collective-permute-done((bf16[512,256]{1,0:T(8,128)(2,1)S(1)}, bf16[512,256]{1,0:T(8,128)(2,1)S(1)}, u32[]{:S(2)}, u32[]{:S(2)}) %collective-permute-start.1) | collective-permute-done | bytes 262176 | tf_op jit(solution)/shard_map/while/body/eval_jaxpr/ppermute | solution.py:19
  67.0 13.0 %collective-permute-start.1 = (bf16[512,256]{1,0:T(8,128)(2,1)S(1)}, bf16[512,256]{1,0:T(8,128)(2,1)S(1)}, u32[]{:S(2)}, u32[]{:S(2)}) collective-permute-start(bf16[512,256]{1,0:T(8,128)(2,1)S(1)} %get-tuple-element.443), channel_id=1, source_target_pairs={{28,0},{29,1},{30,2},{31,3},{0,4},{1,5},{2,6},{3,7},{4,8},{5,9},{6... | collective-permute-start | bytes 786440 | tf_op jit(solution)/shard_map/while/body/eval_jaxpr/ppermute | solution.py:19
  80.4 6.2 %collective-permute-done = bf16[512,256]{1,0:T(8,128)(2,1)S(1)} collective-permute-done((bf16[512,256]{1,0:T(8,128)(2,1)S(1)}, bf16[512,256]{1,0:T(8,128)(2,1)S(1)}, u32[]{:S(2)}, u32[]{:S(2)}) %collective-permute-start) | collective-permute-done | bytes 262176 | tf_op jit(solution)/shard_map/while/body/eval_jaxpr/ppermute | solution.py:19
  87.0 4.2 %collective-permute-done.1 = bf16[512,256]{1,0:T(8,128)(2,1)S(1)} collective-permute-done((bf16[512,256]{1,0:T(8,128)(2,1)S(1)}, bf16[512,256]{1,0:T(8,128)(2,1)S(1)}, u32[]{:S(2)}, u32[]{:S(2)}) %collective-permute-start.1) | collective-permute-done | bytes 262176 | tf_op jit(solution)/shard_map/while/body/eval_jaxpr/ppermute | solution.py:19
  93.3 2.5 %collective-permute-start.1 = (bf16[512,256]{1,0:T(8,128)(2,1)S(1)}, bf16[512,256]{1,0:T(8,128)(2,1)S(1)}, u32[]{:S(2)}, u32[]{:S(2)}) collective-permute-start(bf16[512,256]{1,0:T(8,128)(2,1)S(1)} %get-tuple-element.443), channel_id=1, source_target_pairs={{28,0},{29,1},{30,2},{31,3},{0,4},{1,5},{2,6},{3,7},{4,8},{5,9},{6... | collective-permute-start | bytes 786440 | tf_op jit(solution)/shard_map/while/body/eval_jaxpr/ppermute | solution.py:19
  96.2 10.8 %collective-permute-done = bf16[512,256]{1,0:T(8,128)(2,1)S(1)} collective-permute-done((bf16[512,256]{1,0:T(8,128)(2,1)S(1)}, bf16[512,256]{1,0:T(8,128)(2,1)S(1)}, u32[]{:S(2)}, u32[]{:S(2)}) %collective-permute-start) | collective-permute-done | bytes 262176 | tf_op jit(solution)/shard_map/while/body/eval_jaxpr/ppermute | solution.py:19
  109.4 1.5 %collective-permute-start.5 = (bf16[512,256]{1,0:T(8,128)(2,1)S(1)}, bf16[512,256]{1,0:T(8,128)(2,1)S(1)}, u32[]{:S(2)}, u32[]{:S(2)}) collective-permute-start(bf16[512,256]{1,0:T(8,128)(2,1)S(1)} %get-tuple-element.268), channel_id=1, source_target_pairs={{28,0},{29,1},{30,2},{31,3},{0,4},{1,5},{2,6},{3,7},{4,8},{5,9},{6... | collective-permute-start | bytes 786440 | tf_op jit(solution)/shard_map/ppermute | solution.py:19
  111.0 7.4 %collective-permute-done.5 = bf16[512,256]{1,0:T(8,128)(2,1)S(1)} collective-permute-done((bf16[512,256]{1,0:T(8,128)(2,1)S(1)}, bf16[512,256]{1,0:T(8,128)(2,1)S(1)}, u32[]{:S(2)}, u32[]{:S(2)}) %collective-permute-start.5) | collective-permute-done | bytes 262176 | tf_op jit(solution)/shard_map/ppermute | solution.py:19
  119.3 5.6 %fusion.17 = f32[128,4096]{1,0:T(8,128)} fusion(bf16[6,128,4096]{2,1,0:T(8,128)(2,1)} %bitcast.146, f32[512,128,6]{1,0,2:T(8,128)S(1)} %get-tuple-element.342, f32[6,128]{1,0:T(8,128)S(1)} %max.36, f32[6,128,128]{2,1,0:T(8,128)S(1)} %get-tuple-element.266, f32[6,128]{1,0:T(8,128)S(1)} %get-tuple-element.324, f32[6,128]{1,0:T(8,128)S(1)} %get-tuple-element.325, ...), kind=kOutput, calls=%fused_computation.42 | convolution fusion | flops 908197888 | bytes 10494976 | tf_op jit(solution)/shard_map/htd,hde->te/dot_general | solution.py:145
  124.9 2.8 %reshape.556 = bf16[160,4096]{1,0:T(8,128)(2,1)} reshape(bf16[32,5,4096]{2,1,0:T(8,128)(2,1)} %all-to-all-done.1) | data formatting | bytes 2621440 | tf_op jit(solution)/shard_map/reshape | solution.py:78
  127.8 3.3 %multiply_reduce_fusion = (f32[128]{0:T(128)}, bf16[128,4096]{1,0:T(8,128)(2,1)}) fusion(f32[4096]{0:T(1024)S(1)} %copy-done.5, f32[128,4096]{1,0:T(8,128)S(1)} %copy-done.1, bf16[160,4096]{1,0:T(8,128)(2,1)} %reshape.556, s32[160]{0:T(256)S(1)} %compare_select_fusion.8), kind=kOutput, calls=%fused_computation.43 | convolution fusion | flops 170413952 | bytes 4473984 | tf_op jit(solution)/shard_map/dot_general | solution.py:77
  (107 shorter events, 16.4 us)
Async XLA Ops:
  0.6 13.5 %copy-start = (bf16[128,4096]{1,0:T(8,128)(2,1)S(1)}, bf16[128,4096]{1,0:T(8,128)(2,1)}, u32[]{:S(2)}) copy-start(bf16[128,4096]{1,0:T(8,128)(2,1)} %param.10) | copy-start | bytes 3145732
  0.6 14.1 %copy-start.3 = (bf16[128,256]{1,0:T(8,128)(2,1)S(1)}, bf16[128,256]{1,0:T(8,128)(2,1)}, u32[]{:S(2)}) copy-start(bf16[128,256]{1,0:T(8,128)(2,1)} %param.13) | copy-start | bytes 196612
  0.7 14.0 %copy-start.6 = (s32[128]{0:T(128)S(1)}, s32[128]{0:T(128)}, u32[]{:S(2)}) copy-start(s32[128]{0:T(128)} %param.15) | copy-start | bytes 1540
  0.7 22.7 %collective-permute-start.2 = (bf16[128,256]{1,0:T(8,128)(2,1)}, bf16[128,256]{1,0:T(8,128)(2,1)}, u32[]{:S(2)}, u32[]{:S(2)}) collective-permute-start(bf16[128,256]{1,0:T(8,128)(2,1)} %param.13), channel_id=1, source_target_pairs={{29,0},{30,1},{31,2},{0,3},{1,4},{2,5},{3,6},{4,7},{5,8},{6,9},{7,... | collective-permute-start | bytes 196616 | tf_op jit(solution)/shard_map/ppermute | solution.py:19
  1.6 22.6 %collective-permute-start.3 = (bf16[128,256]{1,0:T(8,128)(2,1)}, bf16[128,256]{1,0:T(8,128)(2,1)}, u32[]{:S(2)}, u32[]{:S(2)}) collective-permute-start(bf16[128,256]{1,0:T(8,128)(2,1)} %param.13), channel_id=1, source_target_pairs={{30,0},{31,1},{0,2},{1,3},{2,4},{3,5},{4,6},{5,7},{6,8},{7,9},{8,1... | collective-permute-start | bytes 196616 | tf_op jit(solution)/shard_map/ppermute | solution.py:19
  3.1 22.0 %collective-permute-start.4 = (bf16[128,256]{1,0:T(8,128)(2,1)}, bf16[128,256]{1,0:T(8,128)(2,1)S(1)}, u32[]{:S(2)}, u32[]{:S(2)}) collective-permute-start(bf16[128,256]{1,0:T(8,128)(2,1)} %param.13), channel_id=1, source_target_pairs={{31,0},{0,1},{1,2},{2,3},{3,4},{4,5},{5,6},{6,7},{7,8},{8,9},{9,10... | collective-permute-start | bytes 196616 | tf_op jit(solution)/shard_map/ppermute | solution.py:19
  6.2 11.7 %all-to-all-start = ((bf16[32,1,5]{2,1,0:T(2,128)(2,1)}), bf16[32,1,5]{2,1,0:T(2,128)(2,1)S(1)}, u32[]{:S(2)}, u32[]{:S(2)}) async-start(bf16[32,1,5]{2,1,0:T(2,128)(2,1)} %reshape.572), calls=%async_computation | async-start | bytes 32768 | tf_op jit(solution)/shard_map/all_to_all | solution.py:67
  17.9 107.0 %all-to-all-start.1 = ((bf16[32,5,4096]{2,1,0:T(8,128)(2,1)}), bf16[32,5,4096]{2,1,0:T(8,128)(2,1)}, u32[]{:S(2)}, u32[]{:S(2)}) async-start(bf16[32,5,4096]{2,1,0:T(8,128)(2,1)} %reshape.555), calls=%async_computation.1 | async-start | bytes 4194304 | tf_op jit(solution)/shard_map/all_to_all | solution.py:60
  25.9 0.8 copy-start.4
  26.7 30.4 %collective-permute-start = (bf16[512,256]{1,0:T(8,128)(2,1)S(1)}, bf16[512,256]{1,0:T(8,128)(2,1)S(1)}, u32[]{:S(2)}, u32[]{:S(2)}) collective-permute-start(bf16[512,256]{1,0:T(8,128)(2,1)S(1)} %get-tuple-element.444), channel_id=1, source_target_pairs={{4,0},{5,1},{6,2},{7,3},{8,4},{9,5},{10,6},{11,7},{12,8},{13,9},{1... | collective-permute-start | bytes 786440 | tf_op jit(solution)/shard_map/while/body/eval_jaxpr/ppermute | solution.py:19
  28.2 36.7 %collective-permute-start.1 = (bf16[512,256]{1,0:T(8,128)(2,1)S(1)}, bf16[512,256]{1,0:T(8,128)(2,1)S(1)}, u32[]{:S(2)}, u32[]{:S(2)}) collective-permute-start(bf16[512,256]{1,0:T(8,128)(2,1)S(1)} %get-tuple-element.443), channel_id=1, source_target_pairs={{28,0},{29,1},{30,2},{31,3},{0,4},{1,5},{2,6},{3,7},{4,8},{5,9},{6... | collective-permute-start | bytes 786440 | tf_op jit(solution)/shard_map/while/body/eval_jaxpr/ppermute | solution.py:19
  66.9 19.6 %collective-permute-start = (bf16[512,256]{1,0:T(8,128)(2,1)S(1)}, bf16[512,256]{1,0:T(8,128)(2,1)S(1)}, u32[]{:S(2)}, u32[]{:S(2)}) collective-permute-start(bf16[512,256]{1,0:T(8,128)(2,1)S(1)} %get-tuple-element.444), channel_id=1, source_target_pairs={{4,0},{5,1},{6,2},{7,3},{8,4},{9,5},{10,6},{11,7},{12,8},{13,9},{1... | collective-permute-start | bytes 786440 | tf_op jit(solution)/shard_map/while/body/eval_jaxpr/ppermute | solution.py:19
  67.0 24.1 %collective-permute-start.1 = (bf16[512,256]{1,0:T(8,128)(2,1)S(1)}, bf16[512,256]{1,0:T(8,128)(2,1)S(1)}, u32[]{:S(2)}, u32[]{:S(2)}) collective-permute-start(bf16[512,256]{1,0:T(8,128)(2,1)S(1)} %get-tuple-element.443), channel_id=1, source_target_pairs={{28,0},{29,1},{30,2},{31,3},{0,4},{1,5},{2,6},{3,7},{4,8},{5,9},{6... | collective-permute-start | bytes 786440 | tf_op jit(solution)/shard_map/while/body/eval_jaxpr/ppermute | solution.py:19
  93.2 13.8 %collective-permute-start = (bf16[512,256]{1,0:T(8,128)(2,1)S(1)}, bf16[512,256]{1,0:T(8,128)(2,1)S(1)}, u32[]{:S(2)}, u32[]{:S(2)}) collective-permute-start(bf16[512,256]{1,0:T(8,128)(2,1)S(1)} %get-tuple-element.444), channel_id=1, source_target_pairs={{4,0},{5,1},{6,2},{7,3},{8,4},{9,5},{10,6},{11,7},{12,8},{13,9},{1... | collective-permute-start | bytes 786440 | tf_op jit(solution)/shard_map/while/body/eval_jaxpr/ppermute | solution.py:19
  93.3 14.1 %collective-permute-start.1 = (bf16[512,256]{1,0:T(8,128)(2,1)S(1)}, bf16[512,256]{1,0:T(8,128)(2,1)S(1)}, u32[]{:S(2)}, u32[]{:S(2)}) collective-permute-start(bf16[512,256]{1,0:T(8,128)(2,1)S(1)} %get-tuple-element.443), channel_id=1, source_target_pairs={{28,0},{29,1},{30,2},{31,3},{0,4},{1,5},{2,6},{3,7},{4,8},{5,9},{6... | collective-permute-start | bytes 786440 | tf_op jit(solution)/shard_map/while/body/eval_jaxpr/ppermute | solution.py:19
  109.4 9.0 %collective-permute-start.5 = (bf16[512,256]{1,0:T(8,128)(2,1)S(1)}, bf16[512,256]{1,0:T(8,128)(2,1)S(1)}, u32[]{:S(2)}, u32[]{:S(2)}) collective-permute-start(bf16[512,256]{1,0:T(8,128)(2,1)S(1)} %get-tuple-element.268), channel_id=1, source_target_pairs={{28,0},{29,1},{30,2},{31,3},{0,4},{1,5},{2,6},{3,7},{4,8},{5,9},{6... | collective-permute-start | bytes 786440 | tf_op jit(solution)/shard_map/ppermute | solution.py:19
  118.4 0.7 copy-start.2
  124.9 2.8 %copy-start.1 = (f32[128,4096]{1,0:T(8,128)S(1)}, f32[128,4096]{1,0:T(8,128)}, u32[]{:S(2)}) copy-start(f32[128,4096]{1,0:T(8,128)} %fusion.17) | copy-start | bytes 6291460
  124.9 2.8 %copy-start.5 = (f32[4096]{0:T(1024)S(1)}, f32[4096]{0:T(1024)}, u32[]{:S(2)}) copy-start(f32[4096]{0:T(1024)} %param.17) | copy-start | bytes 49156
where the time goes:
time: 131 us
  waiting for transfers between devices  65 us (50%)
  starting transfers between devices  32.7 us (25%)
  matrix products  16.7 us (13%)
  local copies, waits for them, and re-layouts  9.46 us (7%)
  other arithmetic  5.98 us (5%)
    ppermute x10, waiting for transfers between devices, passed_along(): return lax.ppermute(block, axis, route)  63.9 us
    ppermute x10, starting transfers between devices, passed_along(): return lax.ppermute(block, axis, route)  22.1 us
    all_to_all x1, starting transfers between devices, on_device(): lax.all_to_all(filled.reshape(ctx_count, capacity), 'ctx', split_axis=0,...  5.82 us
    dot_general x1, matrix products, on_device(): jnp.einsum('htd,hde->te', attended, w_out.reshape(query_heads, HEAD, w_ou...  5.57 us
    all_to_all x1, starting transfers between devices, on_device(): lax.all_to_all(outgoing.reshape(ctx_count, capacity, half_width), 'ctx',...  4.76 us
    dot_general x8, matrix products, online_update(): jnp.einsum('htk,kd->htd', exp_terms.astype(jnp.bfloat16), kv_rows[:, head...  4.11 us
    dot_general x1, matrix products, on_device(): jnp.dot(place_match, arrived.reshape(slot_count, half_width), preferred_e...  3.28 us
    dot_general x9, matrix products, online_update(): jnp.einsum('thd,kd->htk', query_rows, kv_rows[:, :head_size], preferred_e...  3.26 us
  transfers between devices with their start and end apart: 12, of which 7 were waited for; matrix products, arithmetic and copies ran while one was open for 20% of the time, Pallas kernels for 0%

commit v1 on v0

v1 whole, which is shorter than its diff:
```python
import functools
import math

import jax
import jax.numpy as jnp
from jax import lax
from jax.experimental import pallas as pl
from jax.experimental.pallas import tpu as pltpu
from jax.sharding import PartitionSpec as P

HEAD = 128
BLOCK = 128
EMPTY = 64.0


neg_big = -1e30


def partner(me, stride):
    return me + stride * (1 - 2 * ((me // stride) % 2))


def attend(anc_ref, q_ref, own_ref, bias_ref, far_ref, kv_all, k_cat, v_cat, att_ref):
    listed = anc_ref.shape[1]
    k_cat[0:BLOCK, :] = own_ref[:, :HEAD]
    v_cat[0:BLOCK, :] = own_ref[:, HEAD:]
    for j in range(listed):
        block = kv_all[jnp.maximum(anc_ref[0, j], 0)]
        rows = slice((j + 1) * BLOCK, (j + 2) * BLOCK)
        k_cat[rows, :] = block[:, :HEAD]
        v_cat[rows, :] = block[:, HEAD:]
    scale = 1.0 / math.sqrt(HEAD)
    for h in range(q_ref.shape[1] // HEAD):
        cols = slice(h * HEAD, (h + 1) * HEAD)
        logits = lax.dot_general(
            q_ref[:, cols],
            k_cat[...],
            (((1,), (1,)), ((), ())),
            preferred_element_type=jnp.float32,
        )
        near = logits[:, :BLOCK] * scale + bias_ref[...]
        far = logits[:, BLOCK:] * scale + far_ref[...]
        logits = jnp.concatenate([near, far], axis=1)
        top = jnp.max(logits, axis=1, keepdims=True)
        terms = jnp.exp(logits - top)
        total = jnp.sum(terms, axis=1, keepdims=True)
        weighted = jnp.dot(
            terms.astype(jnp.bfloat16), v_cat[...], preferred_element_type=jnp.float32
        )
        att_ref[:, cols] = (weighted / total).astype(jnp.bfloat16)


def kernel(
    n,
    anc_ref,
    q_ref,
    own_ref,
    bias_ref,
    far_ref,
    out_ref,
    w_ref,
    arrived_ref,
    proj_ref,
    kv_all,
    k_cat,
    v_cat,
    att_ref,
    w_vmem,
    w_sem,
    mine_sem,
    h_send,
    h_recv,
    z_send,
    f_send,
    kv_recv,
):
    me = lax.axis_index("ctx")
    lead = n // 8
    low = me % 8
    z = me // 8
    core = me % 2
    stride2 = 4 - 2 * core
    stride3 = 2 + 2 * core
    peers = (partner(me, stride2), partner(me, stride3), partner(me, 1))

    w_copy = pltpu.make_async_copy(w_ref, w_vmem, w_sem)
    w_copy.start()
    mine = pltpu.make_async_copy(out_ref.at[me], arrived_ref.at[me], mine_sem)
    mine.start()
    kv_all[me] = own_ref[...]

    barrier = pltpu.get_barrier_semaphore()

    @pl.loop(1, n)
    def _(d):
        pl.semaphore_signal(barrier, inc=1, device_id={"ctx": (me + d) % n})

    pl.semaphore_wait(barrier, n - 1)

    def hidden_copy(d):
        to = (me + d) % n
        return pltpu.make_async_remote_copy(
            src_ref=out_ref.at[to],
            dst_ref=arrived_ref.at[me],
            send_sem=h_send.at[d],
            recv_sem=h_recv.at[me],
            device_id={"ctx": to},
        )

    def send_hidden(first, count):
        @pl.loop(0, count)
        def _(i):
            hidden_copy(first + i).start()

    def kv_copy(block, send_sem, to):
        return pltpu.make_async_remote_copy(
            src_ref=kv_all.at[block],
            dst_ref=kv_all.at[block],
            send_sem=send_sem,
            recv_sem=kv_recv.at[block],
            device_id={"ctx": to},
        )

    def arrive(block):
        kv_copy(block, z_send.at[0], peers[2]).wait_recv()

    def forward(block, hops):
        for hop in hops:
            kv_copy(block, f_send.at[hop, block], peers[hop]).start()

    @pl.loop(1, lead)
    def _(l):
        kv_copy(me, z_send.at[l], ((z + l) % lead) * 8 + low).start()

    forward(me, (0, 1, 2))

    total = n - 1
    at_start = total // 4
    each = (total - at_start) // (2 * lead)
    second = 1 + at_start + each * (lead - 1)
    third = second + each * lead
    send_hidden(1, at_start)

    @pl.loop(1, lead)
    def _(l):
        block = ((z + l) % lead) * 8 + low
        arrive(block)
        forward(block, (0, 1, 2))
        send_hidden(1 + at_start + each * (l - 1), each)

    @pl.loop(0, lead)
    def _(l):
        block = ((z + l) % lead) * 8 + peers[0] % 8
        arrive(block)
        forward(block, (1, 2))
        send_hidden(second + each * l, each)

    send_hidden(third, n - third)
    across = peers[1]

    @pl.loop(0, lead)
    def _(l):
        block = ((z + l) % lead) * 8 + across % 8
        arrive(block)
        forward(block, (2,))

    across2 = partner(across, stride2)

    @pl.loop(0, lead)
    def _(l):
        block = ((z + l) % lead) * 8 + across2 % 8
        arrive(block)
        forward(block, (2,))

    @pl.loop(0, n // 2)
    def _(i):
        arrive(2 * i + 1 - core)

    attend(anc_ref, q_ref, own_ref, bias_ref, far_ref, kv_all, k_cat, v_cat, att_ref)
    w_copy.wait()
    width = w_ref.shape[1]
    tile = math.gcd(width, 512)

    @pl.loop(0, width // tile)
    def _(i):
        cols = pl.ds(pl.multiple_of(i * tile, tile), tile)
        proj_ref[:, cols] = jnp.dot(
            att_ref[...], w_vmem[:, cols], preferred_element_type=jnp.float32
        )

    mine.wait()

    @pl.loop(1, lead)
    def _(l):
        kv_copy(me, z_send.at[l], ((z + l) % lead) * 8 + low).wait_send()

    @pl.loop(0, lead)
    def _(l):
        base = ((z + l) % lead) * 8
        for hop in (0, 1, 2):
            kv_copy(base + low, f_send.at[hop, base + low], peers[hop]).wait_send()
        two = base + peers[0] % 8
        for hop in (1, 2):
            kv_copy(two, f_send.at[hop, two], peers[hop]).wait_send()
        for far in (base + across % 8, base + across2 % 8):
            kv_copy(far, f_send.at[2, far], peers[2]).wait_send()

    @pl.loop(1, n)
    def _(d):
        hidden_copy(d).wait_send()
        source = (me + d) % n
        pltpu.make_async_remote_copy(
            src_ref=out_ref.at[source],
            dst_ref=arrived_ref.at[source],
            send_sem=h_send.at[d],
            recv_sem=h_recv.at[source],
            device_id={"ctx": source},
        ).wait_recv()


def on_device(hidden_in, route, queries, keys_values, ancestors, segments, w_out, w_score):
    tok_rows = hidden_in.shape[0]
    half_width = hidden_in.shape[1]
    n = lax.axis_size("ctx")
    capacity = (tok_rows + n - 1) // n + 1
    slot_count = n * capacity
    dest_shard = route // tok_rows
    earlier = jnp.arange(tok_rows)[:, None] > jnp.arange(tok_rows)[None, :]
    same = dest_shard[:, None] == dest_shard[None, :]
    slot_rank = jnp.sum((earlier & same).astype(jnp.int32), axis=1)
    slot_index = dest_shard * capacity + slot_rank
    slot_match = jnp.arange(slot_count, dtype=jnp.int32)[:, None] == slot_index[None, :]
    vacant = jnp.where(jnp.any(slot_match, axis=1), 0.0, EMPTY)
    outgoing = (
        jnp.dot(slot_match.astype(jnp.bfloat16), hidden_in, preferred_element_type=jnp.float32)
        + vacant[:, None]
    ).astype(jnp.bfloat16)
    lines = capacity * half_width // 128
    outgoing = outgoing.reshape(n, lines, 128)

    position = jnp.arange(tok_rows)
    own_mask = (position[None, :] <= position[:, None]) & (segments[None, :] == segments[:, None])
    bias = jnp.where(own_mask, 0.0, neg_big).astype(jnp.float32)
    far_bias = jnp.repeat(jnp.where(ancestors >= 0, 0.0, neg_big), BLOCK, axis=1)
    far_bias = far_bias.astype(jnp.float32)
    key_count = (1 + ancestors.shape[1]) * BLOCK
    vmem = pl.BlockSpec(memory_space=pltpu.VMEM)
    anywhere = pl.BlockSpec(memory_space=pl.ANY)
    dma = pltpu.SemaphoreType.DMA
    arrived, partial_proj = pl.pallas_call(
        functools.partial(kernel, n),
        out_shape=(
            jax.ShapeDtypeStruct((n, lines, 128), jnp.bfloat16),
            jax.ShapeDtypeStruct((tok_rows, w_out.shape[1]), jnp.float32),
        ),
        in_specs=[pl.BlockSpec(memory_space=pltpu.SMEM)] + [vmem] * 4 + [anywhere] * 2,
        out_specs=(anywhere, vmem),
        scratch_shapes=[
            pltpu.VMEM((n, BLOCK, 2 * HEAD), jnp.bfloat16),
            pltpu.VMEM((key_count, HEAD), jnp.bfloat16),
            pltpu.VMEM((key_count, HEAD), jnp.bfloat16),
            pltpu.VMEM(queries.shape, jnp.bfloat16),
            pltpu.VMEM(w_out.shape, jnp.bfloat16),
            dma,
            dma,
            dma((n,)),
            dma((n,)),
            dma((n // 8,)),
            dma((3, n)),
            dma((n,)),
        ],
        compiler_params=pltpu.CompilerParams(
            collective_id=0, has_side_effects=True, vmem_limit_bytes=48 * 1024 * 1024
        ),
    )(ancestors, queries, keys_values, bias, far_bias, outgoing, w_out)

    rows_in = arrived.reshape(slot_count, half_width)
    held = arrived[:, :: half_width // 128, 0].reshape(slot_count) < 0.5 * EMPTY
    before = jnp.arange(slot_count)[None, :] <= jnp.arange(slot_count)[:, None]
    local_slot = jnp.sum((before & held[None, :]).astype(jnp.int32), axis=1) - 1
    local_slot = jnp.where(held, local_slot, -1)
    place_match = (jnp.arange(tok_rows, dtype=jnp.int32)[:, None] == local_slot[None, :]).astype(
        jnp.bfloat16
    )
    hidden_ctx = jnp.dot(place_match, rows_in, preferred_element_type=jnp.float32)
    projected = partial_proj
    if lax.axis_size("tp") > 1:
        projected = lax.psum_scatter(partial_proj, "tp", scatter_dimension=1, tiled=True)
    hidden_out = (hidden_ctx + projected).astype(jnp.bfloat16)
    score_part = jnp.sum(hidden_out.astype(jnp.float32) * w_score[None, :], axis=1)
    token_scores = lax.psum(score_part, "tp")
    return (hidden_out, token_scores)


def solution(mesh):
    placed = (
        P(("group", "ctx"), "tp"),
        P(("group", "ctx")),
        P(("group", "ctx"), "tp"),
        P(("group", "ctx"), None),
        P(("group", "ctx"), None),
        P(("group", "ctx")),
        P("tp", None),
        P("tp"),
    )
    return jax.shard_map(
        on_device,
        mesh=mesh,
        in_specs=placed,
        out_specs=(P(("group", "ctx"), "tp"), P(("group", "ctx"))),
        check_vma=False,
    )
```

time: 131 us -> 70.4 us (0.54)
  the two profiles are of different devices: /device:TPU:8 before, /device:TPU:11 now
where the time goes in v1:
time: 70.4 us; the launch traced here: 70.1 us
  Pallas kernels  50.8 us (72%)
  local copies, waits for them, and re-layouts  9.78 us (14%)
  matrix products  4.84 us (7%)
  other arithmetic  3.95 us (6%)
  between operations  0.77 us (1%)
    pallas_call x1, Pallas kernels, on_device(): pl.pallas_call(functools.partial(kernel, n), out_shape=(jax.ShapeDtypeStr...  50.8 us
    dot_general x1, matrix products, on_device(): jnp.dot(place_match, rows_in, preferred_element_type=jnp.float32)  3.28 us
    reshape x1, local copies, waits for them, and re-layouts, on_device(): rows_in = arrived.reshape(slot_count, half_width)  3.26 us
    unnamed x16, local copies, waits for them, and re-layouts  2.43 us
    reshape x1, local copies, waits for them, and re-layouts, on_device(): outgoing = outgoing.reshape(n, lines, 128)  2.38 us
    dot_general x1, matrix products, on_device(): jnp.dot(slot_match.astype(jnp.bfloat16), hidden_in, preferred_element_typ...  1.56 us
    slice x1, local copies, waits for them, and re-layouts, on_device(): held = arrived[:, ::half_width // 128, 0].reshape(slot_count) < 0.5 * EMPTY  1.51 us

profile of v1, /device:TPU:11, one launch (start us, length us, event | category | flops | bytes accessed | tf_op | source)
XLA Modules:
  0.0 70.1 jit_solution(17890489174170529981)
XLA Ops:
  0.6 0.0 copy-start
  0.6 0.8 %and_select_fusion = s32[128]{0:T(128)S(1)} fusion(s32[128]{0:T(128)} %param.9), kind=kLoop, calls=%fused_computation.20 | loop fusion | flops 1920 | bytes 1024 | tf_op jit(solution)/shard_map/jit(floor_divide)/jit(_where)/select_n | solution.py:227
  1.4 0.2 convert_reduce_fusion.1
  1.6 0.7 multiply_add_fusion
  2.2 0.1 fusion.3
  2.4 0.7 fusion.9
  3.0 0.1 broadcast_in_dim.52
  3.1 0.8 %fusion.6.bias_ref = f32[128,128]{1,0:T(8,128)S(1)} fusion(s32[128]{0:T(128)} %param.13), kind=kLoop, calls=%fused_computation.17 | loop fusion | flops 65536 | bytes 66048 | tf_op jit(solution)/shard_map/jit(_where)/select_n | solution.py:243
  3.9 0.0 copy-done
  3.9 0.0 copy-start.4
  4.0 0.0 copy-start.5
  4.0 0.0 copy-start.6
  4.0 1.6 %fusion = bf16[160,4096]{1,0:T(8,128)(2,1)} fusion(bf16[128,4096]{1,0:T(8,128)(2,1)S(1)} %copy-done, f32[160]{0:T(256)S(1)} %broadcast_select_fusion, s32[128]{0:T(128)S(1)} %multiply_add_fusion), kind=kOutput, calls=%fused_computation.2 | convolution fusion | flops 169103360 | bytes 2360448 | tf_op jit(solution)/shard_map/dot_general | solution.py:235
  5.5 2.4 %reshape.38.out_ref = bf16[32,160,128]{2,1,0:T(8,128)(2,1)S(1)} reshape(bf16[160,4096]{1,0:T(8,128)(2,1)} %fusion) | data formatting | bytes 2621440 | tf_op jit(solution)/shard_map/reshape | solution.py:239
  7.9 0.0 copy-done.4
  8.0 50.8 %shard_map.95 = (bf16[32,160,128]{2,1,0:T(8,128)(2,1)S(1)}, f32[128,4096]{1,0:T(8,128)S(1)}) custom-call(s32[1,16]{1,0:T(1,128)S(1)} %copy-done.6, bf16[128,768]{1,0:T(8,128)(2,1)S(1)} %copy-done.4, bf16[128,256]{1,0:T(8,128)(2,1)S(1)} %copy-done.5, f32[128,128]{1,0:T(8,128)S(1)} %fusion.6.bias_ref, f32[1,2048]{1,0:T(1,128)S(1)} %bitcast.5, ...), custom_call_target="tpu_custom_call" | custom-call | tf_op jit(solution)/shard_map/pallas_call | solution.py:250
  58.8 1.3 %copy-done.1 = f32[128,4096]{1,0:T(8,128)} copy-done((f32[128,4096]{1,0:T(8,128)}, f32[128,4096]{1,0:T(8,128)S(1)}, u32[]{:S(2)}) %copy-start.1) | copy-done | bytes 2097176
  60.1 1.1 %copy-done.3 = bf16[32,160,128]{2,1,0:T(8,128)(2,1)} copy-done((bf16[32,160,128]{2,1,0:T(8,128)(2,1)}, bf16[32,160,128]{2,1,0:T(8,128)(2,1)S(1)}, u32[]{:S(2)}) %copy-start.3) | copy-done | bytes 1310744
  61.2 1.5 %slice.3 = bf16[32,5,1]{2,1,0:T(8,128)(2,1)S(1)} slice(bf16[32,160,128]{2,1,0:T(8,128)(2,1)} %copy-done.3), slice={[0:32:1], [0:160:32], [0:1:1]} | slice | bytes 640 | tf_op jit(solution)/shard_map/slice | solution.py:278
  62.7 0.6 compare_reduce_fusion
  63.3 0.1 lt.18
  63.4 3.3 %reshape.39 = bf16[160,4096]{1,0:T(8,128)(2,1)} reshape(bf16[32,160,128]{2,1,0:T(8,128)(2,1)} %copy-done.3) | data formatting | bytes 2621440 | tf_op jit(solution)/shard_map/reshape | solution.py:277
  66.7 0.1 convert_reduce_fusion
  66.8 3.3 %multiply_reduce_fusion = (f32[128]{0:T(128)}, bf16[128,4096]{1,0:T(8,128)(2,1)}) fusion(f32[4096]{0:T(1024)S(1)} %copy-done.7, f32[128,4096]{1,0:T(8,128)S(1)} %copy-done.2, bf16[160,4096]{1,0:T(8,128)(2,1)} %reshape.39, s32[160]{0:T(256)S(1)} %add_select_fusion), kind=kOutput, calls=%fused_computation.4 | convolution fusion | flops 170413952 | bytes 4473984 | tf_op jit(solution)/shard_map/dot_general | solution.py:285
  (10 shorter events, 0.0 us)
Async XLA Ops:
  0.6 3.3 %copy-start = (bf16[128,4096]{1,0:T(8,128)(2,1)S(1)}, bf16[128,4096]{1,0:T(8,128)(2,1)}, u32[]{:S(2)}) copy-start(bf16[128,4096]{1,0:T(8,128)(2,1)} %param.8) | copy-start | bytes 3145732
  3.9 4.0 %copy-start.4 = (bf16[128,768]{1,0:T(8,128)(2,1)S(1)}, bf16[128,768]{1,0:T(8,128)(2,1)}, u32[]{:S(2)}) copy-start(bf16[128,768]{1,0:T(8,128)(2,1)} %q_ref.1) | copy-start | bytes 589828
  4.0 4.0 %copy-start.5 = (bf16[128,256]{1,0:T(8,128)(2,1)S(1)}, bf16[128,256]{1,0:T(8,128)(2,1)}, u32[]{:S(2)}) copy-start(bf16[128,256]{1,0:T(8,128)(2,1)} %own_ref.1) | copy-start | bytes 196612
  4.0 4.0 %copy-start.6 = (s32[1,16]{1,0:T(1,128)S(1)}, s32[1,16]{1,0:T(1,128)}, u32[]{:S(2)}) copy-start(s32[1,16]{1,0:T(1,128)} %anc_ref.1) | copy-start | bytes 196
  58.7 1.4 %copy-start.1 = (f32[128,4096]{1,0:T(8,128)}, f32[128,4096]{1,0:T(8,128)S(1)}, u32[]{:S(2)}) copy-start(f32[128,4096]{1,0:T(8,128)S(1)} %get-tuple-element.5) | copy-start | bytes 6291460
  60.1 1.1 %copy-start.3 = (bf16[32,160,128]{2,1,0:T(8,128)(2,1)}, bf16[32,160,128]{2,1,0:T(8,128)(2,1)S(1)}, u32[]{:S(2)}) copy-start(bf16[32,160,128]{2,1,0:T(8,128)(2,1)S(1)} %get-tuple-element.4) | copy-start | bytes 3932164
  61.2 5.7 %copy-start.7 = (f32[4096]{0:T(1024)S(1)}, f32[4096]{0:T(1024)}, u32[]{:S(2)}) copy-start(f32[4096]{0:T(1024)} %param.15) | copy-start | bytes 49156
  61.2 5.7 %copy-start.2 = (f32[128,4096]{1,0:T(8,128)S(1)}, f32[128,4096]{1,0:T(8,128)}, u32[]{:S(2)}) copy-start(f32[128,4096]{1,0:T(8,128)} %copy-done.1) | copy-start | bytes 6291460

commit v2 on v1

--- a/solution.py
+++ b/solution.py
@@ -20,7 +20,63 @@
     return me + stride * (1 - 2 * ((me // stride) % 2))
 
 
-def attend(anc_ref, q_ref, own_ref, bias_ref, far_ref, kv_all, k_cat, v_cat, att_ref):
+def upright(row):
+    return jnp.transpose(jnp.broadcast_to(row, (row.shape[1], row.shape[1])))
+
+
+def iota(shape, axis):
+    return lax.broadcasted_iota(jnp.int32, shape, axis)
+
+
+def pack(n, capacity, route_ref, hid, spread, out_v):
+    rows, width = hid.shape
+    chunks = width // 128
+    slots = n * capacity
+    dest = (route_ref[...] // rows).astype(jnp.float32)
+    square = (rows, rows)
+    ahead = (upright(dest) == dest) & (iota(square, 0) < iota(square, 1))
+    rank = jnp.sum(jnp.where(ahead, 1.0, 0.0), axis=0, keepdims=True)
+    slot = (dest * capacity + rank).astype(jnp.int32)
+    match = jnp.where(iota((slots, rows), 0) == slot, 1.0, 0.0)
+    vacant = EMPTY * (1.0 - jnp.sum(match, axis=1, keepdims=True))
+    match = match.astype(jnp.bfloat16)
+    for first in range(0, chunks, 4):
+        many = min(4, chunks - first)
+        part = hid[:, first * 128 : (first + many) * 128]
+        part = jnp.dot(match, part, preferred_element_type=jnp.float32) + vacant
+        for c in range(many):
+            spread[pl.ds(first + c, slots, stride=chunks), :] = part[:, c * 128 : (c + 1) * 128]
+    lines = capacity * chunks
+
+    @pl.loop(0, n)
+    def _(i):
+        out_v[i] = spread[pl.ds(pl.multiple_of(i * lines, lines), lines), :].astype(jnp.bfloat16)
+
+
+def placement(slots, rows, first):
+    held = jnp.where(first < 0.5 * EMPTY, 1.0, 0.0).astype(jnp.bfloat16)
+    shape = (slots, slots)
+    upper = jnp.where(iota(shape, 0) <= iota(shape, 1), 1.0, 0.0).astype(jnp.bfloat16)
+    unit = jnp.where(iota(shape, 0) == iota(shape, 1), 1.0, 0.0).astype(jnp.bfloat16)
+    turned = (((0,), (0,)), ((), ()))
+    count = lax.dot_general(held, upper, turned, preferred_element_type=jnp.float32)
+    here = lax.dot_general(held, unit, turned, preferred_element_type=jnp.float32)
+    spot = iota((rows, slots), 0).astype(jnp.float32) + 1.0
+    return jnp.where(count == spot, here, 0.0).astype(jnp.bfloat16)
+
+
+def attend(anc_ref, q_ref, own_ref, seg_ref, kv_all, k_cat, v_cat, att_ref):
+    seg = seg_ref[...].astype(jnp.float32)
+    square = (BLOCK, BLOCK)
+    own_mask = (upright(seg) == seg) & (iota(square, 1) <= iota(square, 0))
+    near_bias = jnp.where(own_mask, 0.0, neg_big)
+    far_bias = jnp.concatenate(
+        [
+            jnp.full((1, BLOCK), jnp.where(anc_ref[0, j] >= 0, 0.0, neg_big), jnp.float32)
+            for j in range(anc_ref.shape[1])
+        ],
+        axis=1,
+    )
     listed = anc_ref.shape[1]
     k_cat[0:BLOCK, :] = own_ref[:, :HEAD]
     v_cat[0:BLOCK, :] = own_ref[:, HEAD:]
@@ -38,8 +94,8 @@
             (((1,), (1,)), ((), ())),
             preferred_element_type=jnp.float32,
         )
-        near = logits[:, :BLOCK] * scale + bias_ref[...]
-        far = logits[:, BLOCK:] * scale + far_ref[...]
+        near = logits[:, :BLOCK] * scale + near_bias
+        far = logits[:, BLOCK:] * scale + far_bias
         logits = jnp.concatenate([near, far], axis=1)
         top = jnp.max(logits, axis=1, keepdims=True)
         terms = jnp.exp(logits - top)
@@ -52,22 +108,31 @@
 
 def kernel(
     n,
+    capacity,
+    finish,
     anc_ref,
     q_ref,
     own_ref,
-    bias_ref,
-    far_ref,
+    route_ref,
+    seg_ref,
+    score_w_ref,
+    hid_ref,
+    w_ref,
+    hidden_ref,
+    second_ref,
     out_ref,
-    w_ref,
     arrived_ref,
-    proj_ref,
+    spread,
+    landed,
+    hid,
+    proj_v,
     kv_all,
     k_cat,
     v_cat,
     att_ref,
     w_vmem,
     w_sem,
-    mine_sem,
+    hid_sem,
     h_send,
     h_recv,
     z_send,
@@ -85,8 +150,8 @@
 
     w_copy = pltpu.make_async_copy(w_ref, w_vmem, w_sem)
     w_copy.start()
-    mine = pltpu.make_async_copy(out_ref.at[me], arrived_ref.at[me], mine_sem)
-    mine.start()
+    hid_copy = pltpu.make_async_copy(hid_ref, hid, hid_sem)
+    hid_copy.start()
     kv_all[me] = own_ref[...]
 
     barrier = pltpu.get_barrier_semaphore()
@@ -97,8 +162,11 @@
 
     pl.semaphore_wait(barrier, n - 1)
 
+    def shift(d):
+        return (d * 11) % n
+
     def hidden_copy(d):
-        to = (me + d) % n
+        to = (me + shift(d)) % n
         return pltpu.make_async_remote_copy(
             src_ref=out_ref.at[to],
             dst_ref=arrived_ref.at[me],
@@ -139,6 +207,8 @@
     each = (total - at_start) // (2 * lead)
     second = 1 + at_start + each * (lead - 1)
     third = second + each * lead
+    hid_copy.wait()
+    pack(n, capacity, route_ref, hid, spread, out_ref)
     send_hidden(1, at_start)
 
     @pl.loop(1, lead)
@@ -176,19 +246,18 @@
     def _(i):
         arrive(2 * i + 1 - core)
 
-    attend(anc_ref, q_ref, own_ref, bias_ref, far_ref, kv_all, k_cat, v_cat, att_ref)
+    attend(anc_ref, q_ref, own_ref, seg_ref, kv_all, k_cat, v_cat, att_ref)
     w_copy.wait()
     width = w_ref.shape[1]
     tile = math.gcd(width, 512)
+    proj_to = proj_v if finish else second_ref
 
     @pl.loop(0, width // tile)
     def _(i):
         cols = pl.ds(pl.multiple_of(i * tile, tile), tile)
-        proj_ref[:, cols] = jnp.dot(
+        proj_to[:, cols] = jnp.dot(
             att_ref[...], w_vmem[:, cols], preferred_element_type=jnp.float32
         )
-
-    mine.wait()
 
     @pl.loop(1, lead)
     def _(l):
@@ -205,10 +274,13 @@
         for far in (base + across % 8, base + across2 % 8):
             kv_copy(far, f_send.at[2, far], peers[2]).wait_send()
 
+    lines = out_ref.shape[1]
+    own_lines = pl.ds(pl.multiple_of(me * lines, lines), lines)
+    landed[own_lines, :] = spread[own_lines, :]
+
     @pl.loop(1, n)
     def _(d):
-        hidden_copy(d).wait_send()
-        source = (me + d) % n
+        source = (me + n - shift(d)) % n
         pltpu.make_async_remote_copy(
             src_ref=out_ref.at[source],
             dst_ref=arrived_ref.at[source],
@@ -216,6 +288,36 @@
             recv_sem=h_recv.at[source],
             device_id={"ctx": source},
         ).wait_recv()
+        landed[pl.ds(pl.multiple_of(source * lines, lines), lines), :] = arrived_ref[
+            source
+        ].astype(jnp.float32)
+
+    rows, held_width = hid.shape
+    chunks = held_width // 128
+    slots = n * capacity
+
+    def column(c):
+        return landed[pl.ds(c, slots, stride=chunks), :]
+
+    place = placement(slots, rows, column(0))
+    tally = jnp.zeros((rows, 128), jnp.float32)
+    for first in range(0, chunks, 2):
+        many = min(2, chunks - first)
+        part = jnp.concatenate([column(first + c) for c in range(many)], axis=1)
+        part = jnp.dot(place, part.astype(jnp.bfloat16), preferred_element_type=jnp.float32)
+        cols = slice(first * 128, (first + many) * 128)
+        if finish:
+            part = (part + proj_v[:, cols]).astype(jnp.bfloat16)
+            scored = part.astype(jnp.float32) * score_w_ref[:, cols]
+            for c in range(many):
+                tally = tally + scored[:, c * 128 : (c + 1) * 128]
+        hidden_ref[:, cols] = part.astype(jnp.bfloat16)
+    if finish:
+        second_ref[...] = jnp.sum(jnp.transpose(tally), axis=0, keepdims=True)
+
+    @pl.loop(1, n)
+    def _(d):
+        hidden_copy(d).wait_send()
 
 
 def on_device(hidden_in, route, queries, keys_values, ancestors, segments, w_out, w_score):
@@ -223,39 +325,28 @@
     half_width = hidden_in.shape[1]
     n = lax.axis_size("ctx")
     capacity = (tok_rows + n - 1) // n + 1
-    slot_count = n * capacity
-    dest_shard = route // tok_rows
-    earlier = jnp.arange(tok_rows)[:, None] > jnp.arange(tok_rows)[None, :]
-    same = dest_shard[:, None] == dest_shard[None, :]
-    slot_rank = jnp.sum((earlier & same).astype(jnp.int32), axis=1)
-    slot_index = dest_shard * capacity + slot_rank
-    slot_match = jnp.arange(slot_count, dtype=jnp.int32)[:, None] == slot_index[None, :]
-    vacant = jnp.where(jnp.any(slot_match, axis=1), 0.0, EMPTY)
-    outgoing = (
-        jnp.dot(slot_match.astype(jnp.bfloat16), hidden_in, preferred_element_type=jnp.float32)
-        + vacant[:, None]
-    ).astype(jnp.bfloat16)
+    finish = lax.axis_size("tp") == 1
     lines = capacity * half_width // 128
-    outgoing = outgoing.reshape(n, lines, 128)
-
-    position = jnp.arange(tok_rows)
-    own_mask = (position[None, :] <= position[:, None]) & (segments[None, :] == segments[:, None])
-    bias = jnp.where(own_mask, 0.0, neg_big).astype(jnp.float32)
-    far_bias = jnp.repeat(jnp.where(ancestors >= 0, 0.0, neg_big), BLOCK, axis=1)
-    far_bias = far_bias.astype(jnp.float32)
     key_count = (1 + ancestors.shape[1]) * BLOCK
     vmem = pl.BlockSpec(memory_space=pltpu.VMEM)
     anywhere = pl.BlockSpec(memory_space=pl.ANY)
     dma = pltpu.SemaphoreType.DMA
-    arrived, partial_proj = pl.pallas_call(
-        functools.partial(kernel, n),
+    wide = (tok_rows, w_out.shape[1])
+    hidden, second = pl.pallas_call(
+        functools.partial(kernel, n, capacity, finish),
         out_shape=(
-            jax.ShapeDtypeStruct((n, lines, 128), jnp.bfloat16),
-            jax.ShapeDtypeStruct((tok_rows, w_out.shape[1]), jnp.float32),
+            jax.ShapeDtypeStruct((tok_rows, half_width), jnp.bfloat16),
+            jax.ShapeDtypeStruct((1, tok_rows) if finish else wide, jnp.float32),
         ),
-        in_specs=[pl.BlockSpec(memory_space=pltpu.SMEM)] + [vmem] * 4 + [anywhere] * 2,
-        out_specs=(anywhere, vmem),
+        in_specs=[pl.BlockSpec(memory_space=pltpu.SMEM)] + [vmem] * 5 + [anywhere] * 2,
+        out_specs=(vmem, vmem),
         scratch_shapes=[
+            pltpu.VMEM((n, lines, 128), jnp.bfloat16),
+            pltpu.VMEM((n, lines, 128), jnp.bfloat16),
+            pltpu.VMEM((n * lines, 128), jnp.float32),
+            pltpu.VMEM((n * lines, 128), jnp.float32),
+            pltpu.VMEM(hidden_in.shape, jnp.bfloat16),
+            pltpu.VMEM(wide if finish else (8, 128), jnp.float32),
             pltpu.VMEM((n, BLOCK, 2 * HEAD), jnp.bfloat16),
             pltpu.VMEM((key_count, HEAD), jnp.bfloat16),
             pltpu.VMEM((key_count, HEAD), jnp.bfloat16),
@@ -272,24 +363,22 @@
         compiler_params=pltpu.CompilerParams(
             collective_id=0, has_side_effects=True, vmem_limit_bytes=48 * 1024 * 1024
         ),
-    )(ancestors, queries, keys_values, bias, far_bias, outgoing, w_out)
-
-    rows_in = arrived.reshape(slot_count, half_width)
-    held = arrived[:, :: half_width // 128, 0].reshape(slot_count) < 0.5 * EMPTY
-    before = jnp.arange(slot_count)[None, :] <= jnp.arange(slot_count)[:, None]
-    local_slot = jnp.sum((before & held[None, :]).astype(jnp.int32), axis=1) - 1
-    local_slot = jnp.where(held, local_slot, -1)
-    place_match = (jnp.arange(tok_rows, dtype=jnp.int32)[:, None] == local_slot[None, :]).astype(
-        jnp.bfloat16
+    )(
+        ancestors,
+        queries,
+        keys_values,
+        route.reshape(1, tok_rows),
+        segments.reshape(1, tok_rows),
+        w_score.reshape(1, w_score.shape[0]),
+        hidden_in,
+        w_out,
     )
-    hidden_ctx = jnp.dot(place_match, rows_in, preferred_element_type=jnp.float32)
-    projected = partial_proj
-    if lax.axis_size("tp") > 1:
-        projected = lax.psum_scatter(partial_proj, "tp", scatter_dimension=1, tiled=True)
-    hidden_out = (hidden_ctx + projected).astype(jnp.bfloat16)
+    if finish:
+        return (hidden, second.reshape(tok_rows))
+    projected = lax.psum_scatter(second, "tp", scatter_dimension=1, tiled=True)
+    hidden_out = (hidden.astype(jnp.float32) + projected).astype(jnp.bfloat16)
     score_part = jnp.sum(hidden_out.astype(jnp.float32) * w_score[None, :], axis=1)
-    token_scores = lax.psum(score_part, "tp")
-    return (hidden_out, token_scores)
+    return (hidden_out, lax.psum(score_part, "tp"))
 
 
 def solution(mesh):

time: 70.4 us -> 54 us (0.77)
  the two profiles are of different devices: /device:TPU:11 before, /device:TPU:0 now
where the time goes in v2:
time: 54 us; the launch traced here: 53.7 us
  Pallas kernels  45.9 us (85%)
  local copies, waits for them, and re-layouts  7.15 us (13%)
  between operations  0.66 us (1%)
    pallas_call x1, Pallas kernels, on_device(): pl.pallas_call(functools.partial(kernel, n, capacity, finish), out_shape=...  45.9 us
    unnamed x16, local copies, waits for them, and re-layouts  7.15 us

profile of v2, /device:TPU:0, one launch (start us, length us, event | category | flops | bytes accessed | tf_op | source)
XLA Modules:
  0.0 53.7 jit_solution(6386609660495274124)
XLA Ops:
  0.6 0.0 copy-start
  0.6 1.2 %copy-done = bf16[128,4096]{1,0:T(8,128)(2,1)S(1)} copy-done((bf16[128,4096]{1,0:T(8,128)(2,1)S(1)}, bf16[128,4096]{1,0:T(8,128)(2,1)}, u32[]{:S(2)}) %copy-start) | copy-done | bytes 1048600
  1.9 0.0 copy-start.1
  1.9 0.9 %copy-done.1 = bf16[128,768]{1,0:T(8,128)(2,1)S(1)} copy-done((bf16[128,768]{1,0:T(8,128)(2,1)S(1)}, bf16[128,768]{1,0:T(8,128)(2,1)}, u32[]{:S(2)}) %copy-start.1) | copy-done | bytes 196632
  2.8 0.0 copy-start.2
  2.8 0.8 %copy-done.2 = bf16[128,256]{1,0:T(8,128)(2,1)S(1)} copy-done((bf16[128,256]{1,0:T(8,128)(2,1)S(1)}, bf16[128,256]{1,0:T(8,128)(2,1)}, u32[]{:S(2)}) %copy-start.2) | copy-done | bytes 65560
  3.6 0.0 copy-start.3
  3.6 0.7 %copy-done.3 = f32[4096]{0:T(1024)S(1)} copy-done((f32[4096]{0:T(1024)S(1)}, f32[4096]{0:T(1024)}, u32[]{:S(2)}) %copy-start.3) | copy-done | bytes 16408
  4.3 0.0 copy-start.4
  4.3 0.7 %copy-done.4 = s32[1,16]{1,0:T(1,128)S(1)} copy-done((s32[1,16]{1,0:T(1,128)S(1)}, s32[1,16]{1,0:T(1,128)}, u32[]{:S(2)}) %copy-start.4) | copy-done | bytes 88
  5.0 0.0 copy-start.5
  5.0 0.7 %copy-done.5 = s32[128]{0:T(128)S(1)} copy-done((s32[128]{0:T(128)S(1)}, s32[128]{0:T(128)}, u32[]{:S(2)}) %copy-start.5) | copy-done | bytes 536
  5.7 0.0 copy-start.6
  5.7 0.7 %copy-done.6 = s32[128]{0:T(128)S(1)} copy-done((s32[128]{0:T(128)S(1)}, s32[128]{0:T(128)}, u32[]{:S(2)}) %copy-start.6) | copy-done | bytes 536
  6.3 45.9 %shard_map.95 = (bf16[128,4096]{1,0:T(8,128)(2,1)S(1)}, f32[1,128]{1,0:T(1,128)S(1)}) custom-call(s32[1,16]{1,0:T(1,128)S(1)} %copy-done.4, bf16[128,768]{1,0:T(8,128)(2,1)S(1)} %copy-done.1, bf16[128,256]{1,0:T(8,128)(2,1)S(1)} %copy-done.2, s32[1,128]{1,0:T(1,128)S(1)} %bitcast.5, s32[1,128]{1,0:T(1,128)S(1)} %bitcast.6, f32[1,4096]{1,0:T(1,128)S(1)} %bitcast.4, ...), custom_call_target="tpu_custom_call" | custom-call | tf_op jit(solution)/shard_map/pallas_call | solution.py:335
  52.2 1.0 %copy.12 = bf16[128,4096]{1,0:T(8,128)(2,1)} copy(bf16[128,4096]{1,0:T(8,128)(2,1)S(1)} %get-tuple-element.8) | data formatting | bytes 2097152
  53.2 0.5 copy.13
Async XLA Ops:
  0.6 1.2 %copy-start = (bf16[128,4096]{1,0:T(8,128)(2,1)S(1)}, bf16[128,4096]{1,0:T(8,128)(2,1)}, u32[]{:S(2)}) copy-start(bf16[128,4096]{1,0:T(8,128)(2,1)} %hid_ref.1) | copy-start | bytes 3145732
  1.9 0.9 %copy-start.1 = (bf16[128,768]{1,0:T(8,128)(2,1)S(1)}, bf16[128,768]{1,0:T(8,128)(2,1)}, u32[]{:S(2)}) copy-start(bf16[128,768]{1,0:T(8,128)(2,1)} %q_ref.1) | copy-start | bytes 589828
  2.8 0.8 %copy-start.2 = (bf16[128,256]{1,0:T(8,128)(2,1)S(1)}, bf16[128,256]{1,0:T(8,128)(2,1)}, u32[]{:S(2)}) copy-start(bf16[128,256]{1,0:T(8,128)(2,1)} %own_ref.1) | copy-start | bytes 196612
  3.6 0.7 %copy-start.3 = (f32[4096]{0:T(1024)S(1)}, f32[4096]{0:T(1024)}, u32[]{:S(2)}) copy-start(f32[4096]{0:T(1024)} %param.15) | copy-start | bytes 49156
  4.3 0.7 %copy-start.4 = (s32[1,16]{1,0:T(1,128)S(1)}, s32[1,16]{1,0:T(1,128)}, u32[]{:S(2)}) copy-start(s32[1,16]{1,0:T(1,128)} %anc_ref.1) | copy-start | bytes 196
  5.0 0.7 %copy-start.5 = (s32[128]{0:T(128)S(1)}, s32[128]{0:T(128)}, u32[]{:S(2)}) copy-start(s32[128]{0:T(128)} %param.9) | copy-start | bytes 1540
  5.7 0.7 %copy-start.6 = (s32[128]{0:T(128)S(1)}, s32[128]{0:T(128)}, u32[]{:S(2)}) copy-start(s32[128]{0:T(128)} %param.13) | copy-start | bytes 1540

commit v3 on v2

--- a/solution.py
+++ b/solution.py
@@ -111,12 +111,12 @@
     capacity,
     finish,
     anc_ref,
-    q_ref,
-    own_ref,
-    route_ref,
-    seg_ref,
-    score_w_ref,
-    hid_ref,
+    q_in,
+    own_in,
+    route_in,
+    seg_in,
+    score_w_in,
+    hid_in,
     w_ref,
     hidden_ref,
     second_ref,
@@ -131,8 +131,13 @@
     v_cat,
     att_ref,
     w_vmem,
+    q_ref,
+    own_ref,
+    route_ref,
+    seg_ref,
+    score_w_ref,
     w_sem,
-    hid_sem,
+    in_sem,
     h_send,
     h_recv,
     z_send,
@@ -148,11 +153,24 @@
     stride3 = 2 + 2 * core
     peers = (partner(me, stride2), partner(me, stride3), partner(me, 1))
 
+    own_copy, route_copy, hid_copy, q_copy, seg_copy, score_copy = [
+        pltpu.make_async_copy(source, target, in_sem.at[i])
+        for i, (source, target) in enumerate(
+            [
+                (own_in, own_ref),
+                (route_in, route_ref),
+                (hid_in, hid),
+                (q_in, q_ref),
+                (seg_in, seg_ref),
+                (score_w_in, score_w_ref),
+            ]
+        )
+    ]
+    early = (own_copy, route_copy, hid_copy, q_copy, seg_copy, score_copy)
+    for copy in early:
+        copy.start()
     w_copy = pltpu.make_async_copy(w_ref, w_vmem, w_sem)
     w_copy.start()
-    hid_copy = pltpu.make_async_copy(hid_ref, hid, hid_sem)
-    hid_copy.start()
-    kv_all[me] = own_ref[...]
 
     barrier = pltpu.get_barrier_semaphore()
 
@@ -160,6 +178,8 @@
     def _(d):
         pl.semaphore_signal(barrier, inc=1, device_id={"ctx": (me + d) % n})
 
+    own_copy.wait()
+    kv_all[me] = own_ref[...]
     pl.semaphore_wait(barrier, n - 1)
 
     def shift(d):
@@ -207,6 +227,7 @@
     each = (total - at_start) // (2 * lead)
     second = 1 + at_start + each * (lead - 1)
     third = second + each * lead
+    route_copy.wait()
     hid_copy.wait()
     pack(n, capacity, route_ref, hid, spread, out_ref)
     send_hidden(1, at_start)
@@ -246,6 +267,8 @@
     def _(i):
         arrive(2 * i + 1 - core)
 
+    q_copy.wait()
+    seg_copy.wait()
     attend(anc_ref, q_ref, own_ref, seg_ref, kv_all, k_cat, v_cat, att_ref)
     w_copy.wait()
     width = w_ref.shape[1]
@@ -292,6 +315,7 @@
             source
         ].astype(jnp.float32)
 
+    score_copy.wait()
     rows, held_width = hid.shape
     chunks = held_width // 128
     slots = n * capacity
@@ -338,7 +362,7 @@
             jax.ShapeDtypeStruct((tok_rows, half_width), jnp.bfloat16),
             jax.ShapeDtypeStruct((1, tok_rows) if finish else wide, jnp.float32),
         ),
-        in_specs=[pl.BlockSpec(memory_space=pltpu.SMEM)] + [vmem] * 5 + [anywhere] * 2,
+        in_specs=[pl.BlockSpec(memory_space=pltpu.SMEM)] + [anywhere] * 7,
         out_specs=(vmem, vmem),
         scratch_shapes=[
             pltpu.VMEM((n, lines, 128), jnp.bfloat16),
@@ -352,8 +376,13 @@
             pltpu.VMEM((key_count, HEAD), jnp.bfloat16),
             pltpu.VMEM(queries.shape, jnp.bfloat16),
             pltpu.VMEM(w_out.shape, jnp.bfloat16),
+            pltpu.VMEM(queries.shape, jnp.bfloat16),
+            pltpu.VMEM(keys_values.shape, jnp.bfloat16),
+            pltpu.VMEM((1, tok_rows), jnp.int32),
+            pltpu.VMEM((1, tok_rows), jnp.int32),
+            pltpu.VMEM((1, w_score.shape[0]), jnp.float32),
             dma,
-            dma,
+            dma((6,)),
             dma((n,)),
             dma((n,)),
             dma((n // 8,)),
@@ -361,7 +390,7 @@
             dma((n,)),
         ],
         compiler_params=pltpu.CompilerParams(
-            collective_id=0, has_side_effects=True, vmem_limit_bytes=48 * 1024 * 1024
+            collective_id=0, has_side_effects=True, vmem_limit_bytes=60 * 1024 * 1024
         ),
     )(
         ancestors,

time: 54 us -> 51.3 us (0.950)
  local copies, waits for them, and re-layouts: 7.15 us -> 3.4 us
  Pallas kernels: 45.9 us -> 47 us
    unnamed x16 -> x2, local copies, waits for them, and re-layouts: 7.15 us -> 3.4 us
    pallas_call x1, Pallas kernels: 45.9 us -> 47 us  [on_device(): pl.pallas_call(functools.partial(kernel, n, capacity, finish), out_shape=...]
where the time goes in v3:
time: 51.3 us; the launch traced here: 51.1 us
  Pallas kernels  47 us (92%)
  local copies, waits for them, and re-layouts  3.4 us (7%)
  between operations  0.64 us (1%)
    pallas_call x1, Pallas kernels, on_device(): pl.pallas_call(functools.partial(kernel, n, capacity, finish), out_shape=...  47 us
    unnamed x2, local copies, waits for them, and re-layouts  3.4 us

profile of v3, /device:TPU:0, one launch (start us, length us, event | category | flops | bytes accessed | tf_op | source)
XLA Modules:
  0.0 51.1 jit_solution(1712870323926589593)
XLA Ops:
  0.6 47.0 %shard_map.95 = (bf16[128,4096]{1,0:T(8,128)(2,1)}, f32[1,128]{1,0:T(1,128)}) custom-call(s32[1,16]{1,0:T(1,128)} %anc_ref.1, bf16[128,768]{1,0:T(8,128)(2,1)} %q_in.1, bf16[128,256]{1,0:T(8,128)(2,1)} %own_in.1, s32[1,128]{1,0:T(1,128)} %bitcast.5, s32[1,128]{1,0:T(1,128)} %bitcast.6, f32[1,4096]{1,0:T(1,128)} %bitcast.4, bf16[128,4096]{1,0:T(8,128)(2,1)} %hid_in.1, ...), custom_call_target="tpu_custom_call" | custom-call | tf_op jit(solution)/shard_map/pallas_call | solution.py:359
  47.7 2.3 %copy.12 = bf16[128,4096]{1,0:T(8,128)(2,1)} copy(bf16[128,4096]{1,0:T(8,128)(2,1)} %get-tuple-element.8) | data formatting | bytes 2097152
  50.0 1.1 %copy.13 = f32[128]{0:T(128)} copy(f32[128]{0:T(128)} %bitcast.7) | data formatting | bytes 1024

commit v4 on v3

--- a/solution.py
+++ b/solution.py
@@ -183,7 +183,7 @@
     pl.semaphore_wait(barrier, n - 1)
 
     def shift(d):
-        return (d * 11) % n
+        return (d * 5) % n
 
     def hidden_copy(d):
         to = (me + shift(d)) % n

time: 51.3 us -> 50.2 us (0.979)
  Pallas kernels: 47 us -> 45.9 us
    pallas_call x1, Pallas kernels: 47 us -> 45.9 us  [on_device(): pl.pallas_call(functools.partial(kernel, n, capacity, finish), out_shape=...]
where the time goes in v4:
time: 50.2 us; the launch traced here: 49.9 us
  Pallas kernels  45.9 us (91%)
  local copies, waits for them, and re-layouts  3.4 us (7%)
  between operations  0.64 us (1%)
    pallas_call x1, Pallas kernels, on_device(): pl.pallas_call(functools.partial(kernel, n, capacity, finish), out_shape=...  45.9 us
    unnamed x2, local copies, waits for them, and re-layouts  3.4 us

profile of v4, /device:TPU:0, one launch (start us, length us, event | category | flops | bytes accessed | tf_op | source)
XLA Modules:
  0.0 49.9 jit_solution(4363353005761962504)
XLA Ops:
  0.6 45.9 %shard_map.95 = (bf16[128,4096]{1,0:T(8,128)(2,1)}, f32[1,128]{1,0:T(1,128)}) custom-call(s32[1,16]{1,0:T(1,128)} %anc_ref.1, bf16[128,768]{1,0:T(8,128)(2,1)} %q_in.1, bf16[128,256]{1,0:T(8,128)(2,1)} %own_in.1, s32[1,128]{1,0:T(1,128)} %bitcast.5, s32[1,128]{1,0:T(1,128)} %bitcast.6, f32[1,4096]{1,0:T(1,128)} %bitcast.4, bf16[128,4096]{1,0:T(8,128)(2,1)} %hid_in.1, ...), custom_call_target="tpu_custom_call" | custom-call | tf_op jit(solution)/shard_map/pallas_call | solution.py:359
  46.5 2.3 %copy.12 = bf16[128,4096]{1,0:T(8,128)(2,1)} copy(bf16[128,4096]{1,0:T(8,128)(2,1)} %get-tuple-element.8) | data formatting | bytes 2097152
  48.8 1.1 %copy.13 = f32[128]{0:T(128)} copy(f32[128]{0:T(128)} %bitcast.7) | data formatting | bytes 1024
